TPU v7x, 512 devices: a whole 4x4x16 slice. The times are simulated.
512 devices in a mesh: tm: 64 (over y_hi, z, core), space: 8 (over y_lo, x).
Axes of the slice: x: 4, y: 4 (y_hi: 2, y_lo: 2; y = y_hi * 2 + y_lo), z: 16, core: 2. Of those that a mesh axis runs over, the one named last changes fastest.
Arguments:
- snapshots: float32 [64, 2, 1024, 1024], P('tm', None, 'space'), may hold values from 0.5 to 8
- coefficients: float32 [2, 1024, 1024], P(None, 'space'), may hold values from 0.9 to 1.8
Outputs:
- u_scale: float32 [64, 2, 1024, 1024], P('tm', None, 'space')
- v_scale: float32 [64, 2, 1024, 1024], P('tm', None, 'space')
All inputs are finite; a program needn't handle non-finite values.
Results may differ from a plain program's by a relative error of at most 0.00002.
Values sent between devices are 32-bit elements; how exact they have to be, the bound alone decides.
A program may use at most 64 MiB of HBM per device.

v0:
```python
import jax
import jax.numpy as jnp
from jax import lax
from jax.sharding import PartitionSpec as P

PASSES = 4
ITERS = 2


tau_rows = 0.25
tau_side = 0.125


def with_halo(cells, sides, width):
    for axis, dim in sides:
        count = lax.axis_size(axis)
        ends = count - 1
        head = lax.slice_in_dim(cells, 0, width, axis=dim)
        tail = lax.slice_in_dim(cells, cells.shape[dim] - width, cells.shape[dim], axis=dim)
        cells = jnp.concatenate(
            [
                lax.ppermute(tail, axis, [(i, (i + 1) % count) for i in range(ends)]),
                cells,
                lax.ppermute(head, axis, [((i + 1) % count, i) for i in range(ends)]),
            ],
            axis=dim,
        )
    return cells


def from_behind(array, axis, by):
    count = lax.axis_size(axis)
    return lax.ppermute(array, axis, [(i, (i + by) % count) for i in range(count)])


def row_sweep(values, coef_field):
    center = values[:, 1:-1]
    coef_mid = coef_field[:, 1:-1]
    flux_sum = 0.5 * (coef_mid + coef_field[:, 2:]) * (values[:, 2:] - center)
    flux_sum = flux_sum + 0.5 * (coef_mid + coef_field[:, :-2]) * (values[:, :-2] - center)
    return center + tau_rows * flux_sum


def side_sweep(values, coef_field):
    coef_pad = jnp.pad(coef_field, ((1, 1), (0, 0), (1, 1)))
    value_pad = jnp.pad(values, ((1, 1), (0, 0), (1, 1)))
    flux_sum = 0.5 * (coef_field + coef_pad[2:, :, 1:-1]) * (value_pad[2:, :, 1:-1] - values)
    flux_sum = flux_sum + 0.5 * (coef_field + coef_pad[:-2, :, 1:-1]) * (
        value_pad[:-2, :, 1:-1] - values
    )
    flux_sum = flux_sum + 0.5 * (coef_field + coef_pad[1:-1, :, 2:]) * (
        value_pad[1:-1, :, 2:] - values
    )
    flux_sum = flux_sum + 0.5 * (coef_field + coef_pad[1:-1, :, :-2]) * (
        value_pad[1:-1, :, :-2] - values
    )
    return values + tau_side * flux_sum


def row_steps():
    return [pass_idx % 4 in (0, 3) for pass_idx in range(PASSES)]


def apply_kernel(values, coef_wide):
    height = values.shape[1]
    length = coef_wide.shape[1]
    rim_depth = (length - height) // 2
    coef_inner = coef_wide[:, rim_depth - 1 : length - rim_depth + 1]
    coef_mid = coef_inner[:, 1:-1]
    for is_row in row_steps():
        if is_row:
            padded = with_halo(values, (("space", 1),), 1)
            values = row_sweep(padded, coef_inner)
        else:
            values = side_sweep(values, coef_mid)
    return values


def per_device(snapshots, coefficients):
    density = snapshots[0]
    rim_depth = sum((1 for is_row in row_steps() if is_row))
    coef_wide = with_halo(coefficients, (("space", 1),), rim_depth)
    following = from_behind(snapshots, "tm", -1)[0]
    v_part = jnp.ones_like(density)
    u_part = jnp.ones_like(density)
    for iter_idx in range(ITERS):
        u_part = density / apply_kernel(v_part, coef_wide)
        v_part = following / apply_kernel(u_part, coef_wide)
    return (u_part[None], v_part[None])


def solution(mesh):
    placed = (P("tm", None, "space", None), P(None, "space", None))
    return jax.shard_map(
        per_device,
        mesh=mesh,
        in_specs=placed,
        out_specs=(P("tm", None, "space", None), P("tm", None, "space", None)),
        check_vma=False,
    )
```

profile of v0, /device:TPU:8, one launch (start us, length us, event | category | flops | bytes accessed | tf_op | source)
XLA Modules:
  0.0 115.1 jit_solution(16777980286420153481)
XLA Ops:
  0.6 0.9 fusion.188
  1.5 3.4 %collective-permute-start.3 = (f32[2,2,1024]{2,1,0:T(2,128)S(1)}, f32[2,2,1024]{2,1,0:T(2,128)S(1)}, u32[]{:S(2)}, u32[]{:S(2)}) collective-permute-start(f32[2,2,1024]{2,1,0:T(2,128)S(1)} %get-tuple-element.21), channel_id=1, source_target_pairs={{0,1},{1,2},{2,3},{3,4},{4,5},{5,6},{6,7},{8,9},{9,10},{10,11},{11... | collective-permute-start | bytes 49160 | tf_op jit(solution)/shard_map/ppermute | solution.py:22
  4.9 4.6 %collective-permute-start.1 = (f32[2,2,1024]{2,1,0:T(2,128)S(1)}, f32[2,2,1024]{2,1,0:T(2,128)S(1)}, u32[]{:S(2)}, u32[]{:S(2)}) collective-permute-start(f32[2,2,1024]{2,1,0:T(2,128)S(1)} %get-tuple-element.22), channel_id=1, source_target_pairs={{1,0},{2,1},{3,2},{4,3},{5,4},{6,5},{7,6},{9,8},{10,9},{11,10},{12... | collective-permute-start | bytes 49160 | tf_op jit(solution)/shard_map/ppermute | solution.py:24
  9.5 0.0 copy-start
  9.5 2.1 %collective-permute-start.4 = (f32[2,1,1024]{2,1,0:T(1,128)S(1)}, f32[2,1,1024]{2,1,0:T(1,128)S(1)}, u32[]{:S(2)}, u32[]{:S(2)}) collective-permute-start(f32[2,1,1024]{2,1,0:T(1,128)S(1)} %broadcast.39), channel_id=1, source_target_pairs={{0,1},{1,2},{2,3},{3,4},{4,5},{5,6},{6,7},{8,9},{9,10},{10,11},{11... | collective-permute-start | bytes 24584 | tf_op jit(solution)/shard_map/ppermute | solution.py:22
  11.6 6.0 %collective-permute-start.2 = (f32[2,1,1024]{2,1,0:T(1,128)S(1)}, f32[2,1,1024]{2,1,0:T(1,128)S(1)}, u32[]{:S(2)}, u32[]{:S(2)}) collective-permute-start(f32[2,1,1024]{2,1,0:T(1,128)S(1)} %broadcast.39), channel_id=1, source_target_pairs={{1,0},{2,1},{3,2},{4,3},{5,4},{6,5},{7,6},{9,8},{10,9},{11,10},{12... | collective-permute-start | bytes 24584 | tf_op jit(solution)/shard_map/ppermute | solution.py:24
  17.6 0.0 collective-permute-done.4
  17.6 1.3 %collective-permute-done.2 = f32[2,1,1024]{2,1,0:T(1,128)S(1)} collective-permute-done((f32[2,1,1024]{2,1,0:T(1,128)S(1)}, f32[2,1,1024]{2,1,0:T(1,128)S(1)}, u32[]{:S(2)}, u32[]{:S(2)}) %collective-permute-start.2) | collective-permute-done | bytes 8224 | tf_op jit(solution)/shard_map/ppermute | solution.py:24
  19.0 0.0 collective-permute-done.3
  19.0 0.0 collective-permute-done.1
  19.0 2.7 %fusion.4 = f32[2,128,1024]{2,1,0:T(8,128)S(1)} fusion(f32[2,1,1024]{2,1,0:T(1,128)S(1)} %collective-permute-done.2, f32[2,1,1024]{2,1,0:T(1,128)S(1)} %collective-permute-done.4, f32[2,128,1024]{2,1,0:T(8,128)} %param.3, f32[2,2,1024]{2,1,0:T(2,128)S(1)} %collective-permute-done.1, f32[2,2,1024]{2,1,0:T(2,128)S(1)} %collective-permute-done.3), kind=kLoop, calls=%fused_computation.42 | loop fusion | flops 3407872 | bytes 2146304 | tf_op jit(solution)/shard_map/add;broadcast_in_dim | solution.py:41
  21.6 0.0 copy-done
  21.6 1.4 %fusion.21 = (f32[2,128,1024]{2,1,0:T(8,128)S(1)}, f32[2,128,1024]{2,1,0:T(8,128)S(1)}, f32[2,128,1024]{2,1,0:T(8,128)S(1)}, f32[2,128,1024]{2,1,0:T(8,128)S(1)}, f32[2,128,1024]{2,1,0:T(8,128)S(1)}) fusion(f32[2,128,1024]{2,1,0:T(8,128)S(1)} %fusion.4, f32[2,128,1024]{2,1,0:T(8,128)S(1)} %copy-done), kind=kLoop, calls=%fused_computation.59 | loop fusion | flops 5505024 | bytes 7340032 | tf_op jit(solution)/shard_map/add | solution.py:57
  23.1 0.0 copy-start.2
  23.1 0.7 fusion.34
  23.8 6.3 %collective-permute-start.5 = (f32[2,1,1024]{2,1,0:T(1,128)S(1)}, f32[2,1,1024]{2,1,0:T(1,128)S(1)}, u32[]{:S(2)}, u32[]{:S(2)}) collective-permute-start(f32[2,1,1024]{2,1,0:T(1,128)S(1)} %get-tuple-element.19), channel_id=1, source_target_pairs={{1,0},{2,1},{3,2},{4,3},{5,4},{6,5},{7,6},{9,8},{10,9},{11,10},{12... | collective-permute-start | bytes 24584 | tf_op jit(solution)/shard_map/ppermute | solution.py:24
  30.1 1.9 %collective-permute-start.6 = (f32[2,1,1024]{2,1,0:T(1,128)S(1)}, f32[2,1,1024]{2,1,0:T(1,128)S(1)}, u32[]{:S(2)}, u32[]{:S(2)}) collective-permute-start(f32[2,1,1024]{2,1,0:T(1,128)S(1)} %get-tuple-element.20), channel_id=1, source_target_pairs={{0,1},{1,2},{2,3},{3,4},{4,5},{5,6},{6,7},{8,9},{9,10},{10,11},{11... | collective-permute-start | bytes 24584 | tf_op jit(solution)/shard_map/ppermute | solution.py:22
  32.1 0.0 collective-permute-done.5
  32.1 5.7 %collective-permute-done.6 = f32[2,1,1024]{2,1,0:T(1,128)S(1)} collective-permute-done((f32[2,1,1024]{2,1,0:T(1,128)S(1)}, f32[2,1,1024]{2,1,0:T(1,128)S(1)}, u32[]{:S(2)}, u32[]{:S(2)}) %collective-permute-start.6) | collective-permute-done | bytes 8224 | tf_op jit(solution)/shard_map/ppermute | solution.py:22
  37.8 0.0 copy-done.2
  37.8 0.8 fusion.169
  38.6 1.9 %collective-permute-start.7 = (f32[2,1,1024]{2,1,0:T(1,128)S(1)}, f32[2,1,1024]{2,1,0:T(1,128)S(1)}, u32[]{:S(2)}, u32[]{:S(2)}) collective-permute-start(f32[2,1,1024]{2,1,0:T(1,128)S(1)} %get-tuple-element.17), channel_id=1, source_target_pairs={{1,0},{2,1},{3,2},{4,3},{5,4},{6,5},{7,6},{9,8},{10,9},{11,10},{12... | collective-permute-start | bytes 24584 | tf_op jit(solution)/shard_map/ppermute | solution.py:24
  40.5 3.9 %collective-permute-start.8 = (f32[2,1,1024]{2,1,0:T(1,128)S(1)}, f32[2,1,1024]{2,1,0:T(1,128)S(1)}, u32[]{:S(2)}, u32[]{:S(2)}) collective-permute-start(f32[2,1,1024]{2,1,0:T(1,128)S(1)} %get-tuple-element.18), channel_id=1, source_target_pairs={{0,1},{1,2},{2,3},{3,4},{4,5},{5,6},{6,7},{8,9},{9,10},{10,11},{11... | collective-permute-start | bytes 24584 | tf_op jit(solution)/shard_map/ppermute | solution.py:22
  44.4 8.6 %collective-permute-start = (f32[1,2,128,1024]{3,2,1,0:T(8,128)S(1)}, f32[1,2,128,1024]{3,2,1,0:T(8,128)S(1)}, u32[]{:S(2)}, u32[]{:S(2)}) collective-permute-start(f32[1,2,128,1024]{3,2,1,0:T(8,128)S(1)} %copy-done.2), channel_id=1, source_target_pairs={{0,504},{8,0},{16,8},{24,16},{32,24},{40,32},{48,40},{56,48},{64,5... | collective-permute-start | bytes 3145736 | tf_op jit(solution)/shard_map/ppermute | solution.py:33
  53.0 0.0 collective-permute-done.7
  53.0 0.0 collective-permute-done.8
  53.0 0.7 fusion.161
  53.7 0.9 fusion.47
  54.7 0.9 fusion.60
  55.6 4.9 %collective-permute-start.9 = (f32[2,1,1024]{2,1,0:T(1,128)S(1)}, f32[2,1,1024]{2,1,0:T(1,128)S(1)}, u32[]{:S(2)}, u32[]{:S(2)}) collective-permute-start(f32[2,1,1024]{2,1,0:T(1,128)S(1)} %get-tuple-element.15), channel_id=1, source_target_pairs={{1,0},{2,1},{3,2},{4,3},{5,4},{6,5},{7,6},{9,8},{10,9},{11,10},{12... | collective-permute-start | bytes 24584 | tf_op jit(solution)/shard_map/ppermute | solution.py:24
  60.6 1.9 %collective-permute-start.10 = (f32[2,1,1024]{2,1,0:T(1,128)S(1)}, f32[2,1,1024]{2,1,0:T(1,128)S(1)}, u32[]{:S(2)}, u32[]{:S(2)}) collective-permute-start(f32[2,1,1024]{2,1,0:T(1,128)S(1)} %get-tuple-element.16), channel_id=1, source_target_pairs={{0,1},{1,2},{2,3},{3,4},{4,5},{5,6},{6,7},{8,9},{9,10},{10,11},{11... | collective-permute-start | bytes 24584 | tf_op jit(solution)/shard_map/ppermute | solution.py:22
  62.5 0.0 collective-permute-done.9
  62.5 5.7 %collective-permute-done.10 = f32[2,1,1024]{2,1,0:T(1,128)S(1)} collective-permute-done((f32[2,1,1024]{2,1,0:T(1,128)S(1)}, f32[2,1,1024]{2,1,0:T(1,128)S(1)}, u32[]{:S(2)}, u32[]{:S(2)}) %collective-permute-start.10) | collective-permute-done | bytes 8224 | tf_op jit(solution)/shard_map/ppermute | solution.py:22
  68.2 0.0 collective-permute-done
  68.2 0.8 fusion.154
  69.0 2.0 %collective-permute-start.11 = (f32[2,1,1024]{2,1,0:T(1,128)S(1)}, f32[2,1,1024]{2,1,0:T(1,128)S(1)}, u32[]{:S(2)}, u32[]{:S(2)}) collective-permute-start(f32[2,1,1024]{2,1,0:T(1,128)S(1)} %get-tuple-element.13), channel_id=1, source_target_pairs={{1,0},{2,1},{3,2},{4,3},{5,4},{6,5},{7,6},{9,8},{10,9},{11,10},{12... | collective-permute-start | bytes 24584 | tf_op jit(solution)/shard_map/ppermute | solution.py:24
  71.0 3.8 %collective-permute-start.12 = (f32[2,1,1024]{2,1,0:T(1,128)S(1)}, f32[2,1,1024]{2,1,0:T(1,128)S(1)}, u32[]{:S(2)}, u32[]{:S(2)}) collective-permute-start(f32[2,1,1024]{2,1,0:T(1,128)S(1)} %get-tuple-element.14), channel_id=1, source_target_pairs={{0,1},{1,2},{2,3},{3,4},{4,5},{5,6},{6,7},{8,9},{9,10},{10,11},{11... | collective-permute-start | bytes 24584 | tf_op jit(solution)/shard_map/ppermute | solution.py:22
  74.8 0.0 collective-permute-done.11
  74.9 3.8 %collective-permute-done.12 = f32[2,1,1024]{2,1,0:T(1,128)S(1)} collective-permute-done((f32[2,1,1024]{2,1,0:T(1,128)S(1)}, f32[2,1,1024]{2,1,0:T(1,128)S(1)}, u32[]{:S(2)}, u32[]{:S(2)}) %collective-permute-start.12) | collective-permute-done | bytes 8224 | tf_op jit(solution)/shard_map/ppermute | solution.py:22
  78.7 0.7 fusion.146
  79.4 0.9 fusion.73
  80.3 0.9 fusion.86
  81.2 1.9 %collective-permute-start.13 = (f32[2,1,1024]{2,1,0:T(1,128)S(1)}, f32[2,1,1024]{2,1,0:T(1,128)S(1)}, u32[]{:S(2)}, u32[]{:S(2)}) collective-permute-start(f32[2,1,1024]{2,1,0:T(1,128)S(1)} %get-tuple-element.11), channel_id=1, source_target_pairs={{1,0},{2,1},{3,2},{4,3},{5,4},{6,5},{7,6},{9,8},{10,9},{11,10},{12... | collective-permute-start | bytes 24584 | tf_op jit(solution)/shard_map/ppermute | solution.py:24
  83.2 3.9 %collective-permute-start.14 = (f32[2,1,1024]{2,1,0:T(1,128)S(1)}, f32[2,1,1024]{2,1,0:T(1,128)S(1)}, u32[]{:S(2)}, u32[]{:S(2)}) collective-permute-start(f32[2,1,1024]{2,1,0:T(1,128)S(1)} %get-tuple-element.12), channel_id=1, source_target_pairs={{0,1},{1,2},{2,3},{3,4},{4,5},{5,6},{6,7},{8,9},{9,10},{10,11},{11... | collective-permute-start | bytes 24584 | tf_op jit(solution)/shard_map/ppermute | solution.py:22
  87.1 0.0 collective-permute-done.13
  87.1 3.7 %collective-permute-done.14 = f32[2,1,1024]{2,1,0:T(1,128)S(1)} collective-permute-done((f32[2,1,1024]{2,1,0:T(1,128)S(1)}, f32[2,1,1024]{2,1,0:T(1,128)S(1)}, u32[]{:S(2)}, u32[]{:S(2)}) %collective-permute-start.14) | collective-permute-done | bytes 8224 | tf_op jit(solution)/shard_map/ppermute | solution.py:22
  90.8 0.8 fusion.139
  91.6 0.0 copy-start.1
  91.6 1.9 %collective-permute-start.15 = (f32[2,1,1024]{2,1,0:T(1,128)S(1)}, f32[2,1,1024]{2,1,0:T(1,128)S(1)}, u32[]{:S(2)}, u32[]{:S(2)}) collective-permute-start(f32[2,1,1024]{2,1,0:T(1,128)S(1)} %get-tuple-element.9), channel_id=1, source_target_pairs={{1,0},{2,1},{3,2},{4,3},{5,4},{6,5},{7,6},{9,8},{10,9},{11,10},{12... | collective-permute-start | bytes 24584 | tf_op jit(solution)/shard_map/ppermute | solution.py:24
  93.6 4.1 %collective-permute-start.16 = (f32[2,1,1024]{2,1,0:T(1,128)S(1)}, f32[2,1,1024]{2,1,0:T(1,128)S(1)}, u32[]{:S(2)}, u32[]{:S(2)}) collective-permute-start(f32[2,1,1024]{2,1,0:T(1,128)S(1)} %get-tuple-element.10), channel_id=1, source_target_pairs={{0,1},{1,2},{2,3},{3,4},{4,5},{5,6},{6,7},{8,9},{9,10},{10,11},{11... | collective-permute-start | bytes 24584 | tf_op jit(solution)/shard_map/ppermute | solution.py:22
  97.7 0.0 collective-permute-done.15
  97.7 3.5 %collective-permute-done.16 = f32[2,1,1024]{2,1,0:T(1,128)S(1)} collective-permute-done((f32[2,1,1024]{2,1,0:T(1,128)S(1)}, f32[2,1,1024]{2,1,0:T(1,128)S(1)}, u32[]{:S(2)}, u32[]{:S(2)}) %collective-permute-start.16) | collective-permute-done | bytes 8224 | tf_op jit(solution)/shard_map/ppermute | solution.py:22
  101.2 0.7 fusion.131
  101.9 0.0 copy-done.1
  101.9 0.9 fusion.99
  102.8 0.9 fusion.112
  103.8 1.9 %collective-permute-start.17 = (f32[2,1,1024]{2,1,0:T(1,128)S(1)}, f32[2,1,1024]{2,1,0:T(1,128)S(1)}, u32[]{:S(2)}, u32[]{:S(2)}) collective-permute-start(f32[2,1,1024]{2,1,0:T(1,128)S(1)} %get-tuple-element.7), channel_id=1, source_target_pairs={{1,0},{2,1},{3,2},{4,3},{5,4},{6,5},{7,6},{9,8},{10,9},{11,10},{12... | collective-permute-start | bytes 24584 | tf_op jit(solution)/shard_map/ppermute | solution.py:24
  105.7 3.9 %collective-permute-start.18 = (f32[2,1,1024]{2,1,0:T(1,128)S(1)}, f32[2,1,1024]{2,1,0:T(1,128)S(1)}, u32[]{:S(2)}, u32[]{:S(2)}) collective-permute-start(f32[2,1,1024]{2,1,0:T(1,128)S(1)} %get-tuple-element.8), channel_id=1, source_target_pairs={{0,1},{1,2},{2,3},{3,4},{4,5},{5,6},{6,7},{8,9},{9,10},{10,11},{11... | collective-permute-start | bytes 24584 | tf_op jit(solution)/shard_map/ppermute | solution.py:22
  109.7 0.0 collective-permute-done.17
  109.7 3.7 %collective-permute-done.18 = f32[2,1,1024]{2,1,0:T(1,128)S(1)} collective-permute-done((f32[2,1,1024]{2,1,0:T(1,128)S(1)}, f32[2,1,1024]{2,1,0:T(1,128)S(1)}, u32[]{:S(2)}, u32[]{:S(2)}) %collective-permute-start.18) | collective-permute-done | bytes 8224 | tf_op jit(solution)/shard_map/ppermute | solution.py:22
  113.4 1.7 %fusion.176 = f32[1,2,128,1024]{3,2,1,0:T(8,128)} fusion(f32[2,128,1024]{2,1,0:T(8,128)S(1)} %fusion.112, f32[2,1,1024]{2,1,0:T(1,128)S(1)} %collective-permute-done.18, f32[2,1,1024]{2,1,0:T(1,128)S(1)} %collective-permute-done.17, f32[1,2,128,1024]{3,2,1,0:T(8,128)S(1)} %collective-permute-done, f32[2,128,1024]{2,1,0:T(8,128)S(1)} %copy-done, ...), kind=kLoop, calls=%fused_computation.230 | loop fusion | flops 4194304 | bytes 4243456 | tf_op jit(solution)/shard_map/broadcast_in_dim | solution.py:89
  (8 shorter events, 0.1 us)
Async XLA Ops:
  1.5 17.4 %collective-permute-start.3 = (f32[2,2,1024]{2,1,0:T(2,128)S(1)}, f32[2,2,1024]{2,1,0:T(2,128)S(1)}, u32[]{:S(2)}, u32[]{:S(2)}) collective-permute-start(f32[2,2,1024]{2,1,0:T(2,128)S(1)} %get-tuple-element.21), channel_id=1, source_target_pairs={{0,1},{1,2},{2,3},{3,4},{4,5},{5,6},{6,7},{8,9},{9,10},{10,11},{11... | collective-permute-start | bytes 49160 | tf_op jit(solution)/shard_map/ppermute | solution.py:22
  4.9 14.0 %collective-permute-start.1 = (f32[2,2,1024]{2,1,0:T(2,128)S(1)}, f32[2,2,1024]{2,1,0:T(2,128)S(1)}, u32[]{:S(2)}, u32[]{:S(2)}) collective-permute-start(f32[2,2,1024]{2,1,0:T(2,128)S(1)} %get-tuple-element.22), channel_id=1, source_target_pairs={{1,0},{2,1},{3,2},{4,3},{5,4},{6,5},{7,6},{9,8},{10,9},{11,10},{12... | collective-permute-start | bytes 49160 | tf_op jit(solution)/shard_map/ppermute | solution.py:24
  9.5 12.1 %copy-start = (f32[2,128,1024]{2,1,0:T(8,128)S(1)}, f32[2,128,1024]{2,1,0:T(8,128)}, u32[]{:S(2)}) copy-start(f32[2,128,1024]{2,1,0:T(8,128)} %param.3) | copy-start | bytes 3145732
  9.5 8.1 %collective-permute-start.4 = (f32[2,1,1024]{2,1,0:T(1,128)S(1)}, f32[2,1,1024]{2,1,0:T(1,128)S(1)}, u32[]{:S(2)}, u32[]{:S(2)}) collective-permute-start(f32[2,1,1024]{2,1,0:T(1,128)S(1)} %broadcast.39), channel_id=1, source_target_pairs={{0,1},{1,2},{2,3},{3,4},{4,5},{5,6},{6,7},{8,9},{9,10},{10,11},{11... | collective-permute-start | bytes 24584 | tf_op jit(solution)/shard_map/ppermute | solution.py:22
  11.6 7.4 %collective-permute-start.2 = (f32[2,1,1024]{2,1,0:T(1,128)S(1)}, f32[2,1,1024]{2,1,0:T(1,128)S(1)}, u32[]{:S(2)}, u32[]{:S(2)}) collective-permute-start(f32[2,1,1024]{2,1,0:T(1,128)S(1)} %broadcast.39), channel_id=1, source_target_pairs={{1,0},{2,1},{3,2},{4,3},{5,4},{6,5},{7,6},{9,8},{10,9},{11,10},{12... | collective-permute-start | bytes 24584 | tf_op jit(solution)/shard_map/ppermute | solution.py:24
  23.1 14.7 %copy-start.2 = (f32[1,2,128,1024]{3,2,1,0:T(8,128)S(1)}, f32[1,2,128,1024]{3,2,1,0:T(8,128)}, u32[]{:S(2)}) copy-start(f32[1,2,128,1024]{3,2,1,0:T(8,128)} %param.2) | copy-start | bytes 3145732
  23.8 8.2 %collective-permute-start.5 = (f32[2,1,1024]{2,1,0:T(1,128)S(1)}, f32[2,1,1024]{2,1,0:T(1,128)S(1)}, u32[]{:S(2)}, u32[]{:S(2)}) collective-permute-start(f32[2,1,1024]{2,1,0:T(1,128)S(1)} %get-tuple-element.19), channel_id=1, source_target_pairs={{1,0},{2,1},{3,2},{4,3},{5,4},{6,5},{7,6},{9,8},{10,9},{11,10},{12... | collective-permute-start | bytes 24584 | tf_op jit(solution)/shard_map/ppermute | solution.py:24
  30.1 7.7 %collective-permute-start.6 = (f32[2,1,1024]{2,1,0:T(1,128)S(1)}, f32[2,1,1024]{2,1,0:T(1,128)S(1)}, u32[]{:S(2)}, u32[]{:S(2)}) collective-permute-start(f32[2,1,1024]{2,1,0:T(1,128)S(1)} %get-tuple-element.20), channel_id=1, source_target_pairs={{0,1},{1,2},{2,3},{3,4},{4,5},{5,6},{6,7},{8,9},{9,10},{10,11},{11... | collective-permute-start | bytes 24584 | tf_op jit(solution)/shard_map/ppermute | solution.py:22
  38.6 14.5 %collective-permute-start.7 = (f32[2,1,1024]{2,1,0:T(1,128)S(1)}, f32[2,1,1024]{2,1,0:T(1,128)S(1)}, u32[]{:S(2)}, u32[]{:S(2)}) collective-permute-start(f32[2,1,1024]{2,1,0:T(1,128)S(1)} %get-tuple-element.17), channel_id=1, source_target_pairs={{1,0},{2,1},{3,2},{4,3},{5,4},{6,5},{7,6},{9,8},{10,9},{11,10},{12... | collective-permute-start | bytes 24584 | tf_op jit(solution)/shard_map/ppermute | solution.py:24
  40.5 12.5 %collective-permute-start.8 = (f32[2,1,1024]{2,1,0:T(1,128)S(1)}, f32[2,1,1024]{2,1,0:T(1,128)S(1)}, u32[]{:S(2)}, u32[]{:S(2)}) collective-permute-start(f32[2,1,1024]{2,1,0:T(1,128)S(1)} %get-tuple-element.18), channel_id=1, source_target_pairs={{0,1},{1,2},{2,3},{3,4},{4,5},{5,6},{6,7},{8,9},{9,10},{10,11},{11... | collective-permute-start | bytes 24584 | tf_op jit(solution)/shard_map/ppermute | solution.py:22
  44.4 23.8 %collective-permute-start = (f32[1,2,128,1024]{3,2,1,0:T(8,128)S(1)}, f32[1,2,128,1024]{3,2,1,0:T(8,128)S(1)}, u32[]{:S(2)}, u32[]{:S(2)}) collective-permute-start(f32[1,2,128,1024]{3,2,1,0:T(8,128)S(1)} %copy-done.2), channel_id=1, source_target_pairs={{0,504},{8,0},{16,8},{24,16},{32,24},{40,32},{48,40},{56,48},{64,5... | collective-permute-start | bytes 3145736 | tf_op jit(solution)/shard_map/ppermute | solution.py:33
  55.6 6.9 %collective-permute-start.9 = (f32[2,1,1024]{2,1,0:T(1,128)S(1)}, f32[2,1,1024]{2,1,0:T(1,128)S(1)}, u32[]{:S(2)}, u32[]{:S(2)}) collective-permute-start(f32[2,1,1024]{2,1,0:T(1,128)S(1)} %get-tuple-element.15), channel_id=1, source_target_pairs={{1,0},{2,1},{3,2},{4,3},{5,4},{6,5},{7,6},{9,8},{10,9},{11,10},{12... | collective-permute-start | bytes 24584 | tf_op jit(solution)/shard_map/ppermute | solution.py:24
  60.6 7.7 %collective-permute-start.10 = (f32[2,1,1024]{2,1,0:T(1,128)S(1)}, f32[2,1,1024]{2,1,0:T(1,128)S(1)}, u32[]{:S(2)}, u32[]{:S(2)}) collective-permute-start(f32[2,1,1024]{2,1,0:T(1,128)S(1)} %get-tuple-element.16), channel_id=1, source_target_pairs={{0,1},{1,2},{2,3},{3,4},{4,5},{5,6},{6,7},{8,9},{9,10},{10,11},{11... | collective-permute-start | bytes 24584 | tf_op jit(solution)/shard_map/ppermute | solution.py:22
  69.0 5.9 %collective-permute-start.11 = (f32[2,1,1024]{2,1,0:T(1,128)S(1)}, f32[2,1,1024]{2,1,0:T(1,128)S(1)}, u32[]{:S(2)}, u32[]{:S(2)}) collective-permute-start(f32[2,1,1024]{2,1,0:T(1,128)S(1)} %get-tuple-element.13), channel_id=1, source_target_pairs={{1,0},{2,1},{3,2},{4,3},{5,4},{6,5},{7,6},{9,8},{10,9},{11,10},{12... | collective-permute-start | bytes 24584 | tf_op jit(solution)/shard_map/ppermute | solution.py:24
  71.0 7.7 %collective-permute-start.12 = (f32[2,1,1024]{2,1,0:T(1,128)S(1)}, f32[2,1,1024]{2,1,0:T(1,128)S(1)}, u32[]{:S(2)}, u32[]{:S(2)}) collective-permute-start(f32[2,1,1024]{2,1,0:T(1,128)S(1)} %get-tuple-element.14), channel_id=1, source_target_pairs={{0,1},{1,2},{2,3},{3,4},{4,5},{5,6},{6,7},{8,9},{9,10},{10,11},{11... | collective-permute-start | bytes 24584 | tf_op jit(solution)/shard_map/ppermute | solution.py:22
  81.2 5.9 %collective-permute-start.13 = (f32[2,1,1024]{2,1,0:T(1,128)S(1)}, f32[2,1,1024]{2,1,0:T(1,128)S(1)}, u32[]{:S(2)}, u32[]{:S(2)}) collective-permute-start(f32[2,1,1024]{2,1,0:T(1,128)S(1)} %get-tuple-element.11), channel_id=1, source_target_pairs={{1,0},{2,1},{3,2},{4,3},{5,4},{6,5},{7,6},{9,8},{10,9},{11,10},{12... | collective-permute-start | bytes 24584 | tf_op jit(solution)/shard_map/ppermute | solution.py:24
  83.2 7.7 %collective-permute-start.14 = (f32[2,1,1024]{2,1,0:T(1,128)S(1)}, f32[2,1,1024]{2,1,0:T(1,128)S(1)}, u32[]{:S(2)}, u32[]{:S(2)}) collective-permute-start(f32[2,1,1024]{2,1,0:T(1,128)S(1)} %get-tuple-element.12), channel_id=1, source_target_pairs={{0,1},{1,2},{2,3},{3,4},{4,5},{5,6},{6,7},{8,9},{9,10},{10,11},{11... | collective-permute-start | bytes 24584 | tf_op jit(solution)/shard_map/ppermute | solution.py:22
  91.6 10.3 %copy-start.1 = (f32[2,128,1024]{2,1,0:T(8,128)}, f32[2,128,1024]{2,1,0:T(8,128)S(1)}, u32[]{:S(2)}) copy-start(f32[2,128,1024]{2,1,0:T(8,128)S(1)} %fusion.139) | copy-start | bytes 3145732
  91.6 6.0 %collective-permute-start.15 = (f32[2,1,1024]{2,1,0:T(1,128)S(1)}, f32[2,1,1024]{2,1,0:T(1,128)S(1)}, u32[]{:S(2)}, u32[]{:S(2)}) collective-permute-start(f32[2,1,1024]{2,1,0:T(1,128)S(1)} %get-tuple-element.9), channel_id=1, source_target_pairs={{1,0},{2,1},{3,2},{4,3},{5,4},{6,5},{7,6},{9,8},{10,9},{11,10},{12... | collective-permute-start | bytes 24584 | tf_op jit(solution)/shard_map/ppermute | solution.py:24
  93.6 7.7 %collective-permute-start.16 = (f32[2,1,1024]{2,1,0:T(1,128)S(1)}, f32[2,1,1024]{2,1,0:T(1,128)S(1)}, u32[]{:S(2)}, u32[]{:S(2)}) collective-permute-start(f32[2,1,1024]{2,1,0:T(1,128)S(1)} %get-tuple-element.10), channel_id=1, source_target_pairs={{0,1},{1,2},{2,3},{3,4},{4,5},{5,6},{6,7},{8,9},{9,10},{10,11},{11... | collective-permute-start | bytes 24584 | tf_op jit(solution)/shard_map/ppermute | solution.py:22
  103.8 5.9 %collective-permute-start.17 = (f32[2,1,1024]{2,1,0:T(1,128)S(1)}, f32[2,1,1024]{2,1,0:T(1,128)S(1)}, u32[]{:S(2)}, u32[]{:S(2)}) collective-permute-start(f32[2,1,1024]{2,1,0:T(1,128)S(1)} %get-tuple-element.7), channel_id=1, source_target_pairs={{1,0},{2,1},{3,2},{4,3},{5,4},{6,5},{7,6},{9,8},{10,9},{11,10},{12... | collective-permute-start | bytes 24584 | tf_op jit(solution)/shard_map/ppermute | solution.py:24
  105.7 7.7 %collective-permute-start.18 = (f32[2,1,1024]{2,1,0:T(1,128)S(1)}, f32[2,1,1024]{2,1,0:T(1,128)S(1)}, u32[]{:S(2)}, u32[]{:S(2)}) collective-permute-start(f32[2,1,1024]{2,1,0:T(1,128)S(1)} %get-tuple-element.8), channel_id=1, source_target_pairs={{0,1},{1,2},{2,3},{3,4},{4,5},{5,6},{6,7},{8,9},{9,10},{10,11},{11... | collective-permute-start | bytes 24584 | tf_op jit(solution)/shard_map/ppermute | solution.py:22
where the time goes:
time: 116 us; the launch traced here: 115 us
  starting transfers between devices  69.1 us (60%)
  waiting for transfers between devices  27.6 us (24%)
  other arithmetic  16.4 us (14%)
    ppermute x9, starting transfers between devices, with_halo(): lax.ppermute(head, axis, [((i + 1) % count, i) for i in range(ends)])  31.5 us
    ppermute x9, starting transfers between devices, with_halo(): lax.ppermute(tail, axis, [(i, (i + 1) % count) for i in range(ends)])  29 us
    ppermute x9, waiting for transfers between devices, with_halo(): lax.ppermute(tail, axis, [(i, (i + 1) % count) for i in range(ends)])  26.2 us
    ppermute x1, starting transfers between devices, from_behind(): lax.ppermute(array, axis, [(i, (i + by) % count) for i in range(count)])  8.59 us
    add x8, other arithmetic, side_sweep(): return values + tau_side * flux_sum  7.7 us
    another operation x1, other arithmetic, row_sweep(): return center + tau_rows * flux_sum  2.67 us
  transfers between devices with their start and end apart: 19, of which 7 were waited for; matrix products, arithmetic and copies ran while one was open for 2% of the time, Pallas kernels for 0%

commit v1 on v0

v1 whole, which is shorter than its diff:
```python
import jax
import jax.numpy as jnp
from jax import lax
from jax.experimental import pallas as pl
from jax.experimental.pallas import tpu as pltpu
from jax.sharding import PartitionSpec as P

MESH = pl.DeviceIdType.MESH
TILE = 8
LANES = 128
CHUNK_TILES = 2


def body(
    tm, space, snap, coef, u_out, v_out, a_ext, b_ext, c_ext, vals, mids, mids2, recip, g_row, g_col, g_pl, keep, loc_sem, snd, rcv
):
    t, s = lax.axis_index("tm"), lax.axis_index("space")
    ahead, behind = lax.rem(t + 1, tm), lax.rem(t + tm - 1, tm)
    has_up, has_dn = s > 0, s < space - 1
    up, dn = jnp.maximum(s - 1, 0), jnp.minimum(s + 1, space - 1)
    height, width = coef.shape[1], coef.shape[2]
    cols = width // LANES
    tiles = height // TILE + 2
    chunks = height // (TILE * CHUNK_TILES)
    rows = TILE * CHUNK_TILES

    load_a = pltpu.make_async_copy(snap.at[0], a_ext.at[:, pl.ds(TILE, height)], loc_sem.at[0])
    load_c = pltpu.make_async_copy(coef, c_ext.at[:, pl.ds(TILE, height)], loc_sem.at[1])
    load_c.start()
    load_a.start()

    barrier = pltpu.get_barrier_semaphore()

    def greet(dst_t, dst_s):
        pl.semaphore_signal(barrier, inc=1, device_id={"tm": dst_t, "space": dst_s}, device_id_type=MESH)

    greet(ahead, s)

    @pl.when(has_up)
    def _():
        greet(t, up)
        greet(ahead, up)

    @pl.when(has_dn)
    def _():
        greet(t, dn)
        greet(ahead, dn)

    pl.semaphore_wait(barrier, 1 + 2 * has_up.astype(jnp.int32) + 2 * has_dn.astype(jnp.int32))

    def send(i, src, dst, dst_t, dst_s):
        return pltpu.make_async_remote_copy(
            src_ref=src,
            dst_ref=dst,
            send_sem=snd.at[i],
            recv_sem=rcv.at[i],
            device_id={"tm": dst_t, "space": dst_s},
            device_id_type=MESH,
        )

    first, last = pl.ds(0, TILE), pl.ds(height - TILE, TILE)
    head, tail = pl.ds(0, TILE), pl.ds(height + TILE, TILE)
    to_up = [
        send(0, coef.at[:, first], c_ext.at[:, tail], t, up),
        send(1, snap.at[0, :, first], a_ext.at[:, tail], t, up),
        send(2, snap.at[0, :, first], b_ext.at[:, tail], behind, up),
    ]
    to_dn = [
        send(3, coef.at[:, last], c_ext.at[:, head], t, dn),
        send(4, snap.at[0, :, last], a_ext.at[:, head], t, dn),
        send(5, snap.at[0, :, last], b_ext.at[:, head], behind, dn),
    ]
    for n in range(3):

        @pl.when(has_up)
        def _():
            to_up[n].start()

        @pl.when(has_dn)
        def _():
            to_dn[n].start()

    def whole(k):
        return send(
            6 + k,
            snap.at[0, :, pl.ds(k * rows, rows)],
            b_ext.at[:, pl.ds(TILE + k * rows, rows)],
            behind,
            s,
        )

    for k in range(chunks):
        whole(k).start()

    lane = lax.broadcasted_iota(jnp.int32, (TILE, LANES), 1)
    is_first, is_last = lane == 0, lane == LANES - 1

    def at(e, shift=0):
        return pl.ds(TILE * e + TILE + shift, TILE)

    def native(e, j):
        return pl.ds(pl.multiple_of(TILE * e, TILE), TILE), pl.ds(LANES * j, LANES)

    def clear(ref, e):
        for p in range(2):
            for j in range(cols):
                ref[p, j, pl.ds(TILE * e + TILE, TILE), :] = jnp.zeros((TILE, LANES), jnp.float32)

    def clear_ends(ref, lo, hi):
        @pl.when(jnp.logical_and(s == 0, lo == 0))
        def _():
            clear(ref, 0)

        @pl.when(jnp.logical_and(s == space - 1, hi == tiles))
        def _():
            clear(ref, tiles - 1)

    def row_pass(src, p, j, e):
        mid = src[p, j, at(e), :]
        below = g_row[p, j, at(e), :] * (src[p, j, at(e, 1), :] - mid)
        above = g_row[p, j, at(e, -1), :] * (mid - src[p, j, at(e, -1), :])
        return mid + (below - above)

    def side_pass(x, e):
        across = [g_pl[j, at(e), :] * (x[1][j] - x[0][j]) for j in range(cols)]
        out = []
        for p in range(2):
            rolled = [
                pltpu.roll(jnp.where(is_first, x[p][(j + 1) % cols], x[p][j]), LANES - 1, 1) for j in range(cols)
            ]
            flux = [g_col[p, j, at(e), :] * (rolled[j] - x[p][j]) for j in range(cols)]
            back = [pltpu.roll(jnp.where(is_last, flux[j - 1], flux[j]), 1, 1) for j in range(cols)]
            out.append(
                [
                    keep[p, j, at(e), :] * x[p][j] + (flux[j] - back[j]) + (across[j] if p == 0 else -across[j])
                    for j in range(cols)
                ]
            )
        return out

    def first_three(src, dst, lo, hi):
        @pl.loop(lo, hi)
        def _(e):
            x = [[row_pass(src, p, j, e) for j in range(cols)] for p in range(2)]
            x = side_pass(side_pass(x, e), e)
            for p in range(2):
                for j in range(cols):
                    dst[p, j, at(e), :] = x[p][j]

        clear_ends(dst, lo, hi)

    def fourth(src, lo, hi, put):
        @pl.loop(lo, hi)
        def _(e):
            for p in range(2):
                for j in range(cols):
                    put(p, j, e, row_pass(src, p, j, e))

    load_c.wait()

    @pl.when(has_up)
    def _():
        to_dn[0].wait_recv()

    @pl.when(has_dn)
    def _():
        to_up[0].wait_recv()

    @pl.when(s == 0)
    def _():
        c_ext[:, pl.ds(0, TILE), :] = jnp.zeros((2, TILE, width), jnp.float32)

    @pl.when(s == space - 1)
    def _():
        c_ext[:, pl.ds(height + TILE, TILE), :] = jnp.zeros((2, TILE, width), jnp.float32)

    @pl.loop(0, tiles)
    def _(e):
        for p in range(2):
            for j in range(cols):
                g_row[p, j, at(e), :] = c_ext[p, native(e, j)[0], native(e, j)[1]]
                vals[p, j, at(e), :] = jnp.ones((TILE, LANES), jnp.float32)

    clear_ends(vals, 0, tiles)

    @pl.loop(0, tiles)
    def _(e):
        c = [[g_row[p, j, at(e), :] for j in range(cols)] for p in range(2)]
        for j in range(cols):
            g_pl[j, at(e), :] = 0.0625 * (c[0][j] + c[1][j])
        for p in range(2):
            for j in range(cols):
                right = pltpu.roll(jnp.where(is_first, c[p][(j + 1) % cols], c[p][j]), LANES - 1, 1)
                side = 0.0625 * (c[p][j] + right)
                walls = 0.0625 * c[p][j]
                kept = 1.0 - walls
                if j == cols - 1:
                    side = jnp.where(is_last, 0.0, side)
                    kept = jnp.where(is_last, kept - walls, kept)
                if j == 0:
                    kept = jnp.where(is_first, kept - walls, kept)
                g_col[p, j, at(e), :] = side
                keep[p, j, at(e), :] = kept
                g_row[p, j, at(e), :] = 0.125 * (c[p][j] + g_row[p, j, at(e, 1), :])

    first_three(vals, mids, 0, tiles)
    load_a.wait()

    @pl.when(has_up)
    def _():
        to_dn[1].wait_recv()

    @pl.when(has_dn)
    def _():
        to_up[1].wait_recv()

    def put_u(p, j, e, den):
        r, c = native(e, j)
        vals[p, j, at(e), :] = a_ext[p, r, c] / den

    fourth(mids, 0, tiles, put_u)
    clear_ends(vals, 0, tiles)

    first_three(vals, mids, 0, tiles)

    def put_recip(p, j, e, den):
        recip[p, j, at(e), :] = 1.0 / den

    fourth(mids, 0, tiles, put_recip)

    @pl.when(has_up)
    def _():
        to_dn[2].wait_recv()

    @pl.when(has_dn)
    def _():
        to_up[2].wait_recv()

    def put_u_out(p, j, e, den):
        r, c = native(e, j)
        u = a_ext[p, r, c] / den
        vals[p, j, at(e), :] = u
        u_out[p, r, c] = u

    def put_v_out(p, j, e, den):
        r, c = native(e, j)
        v_out[p, r, c] = b_ext[p, r, c] / den

    def bounds(k, stage):
        low = 1 if stage == 4 else 0
        top = tiles - 1 if stage == 4 else tiles

        def reach(n):
            return jnp.where(n == chunks - 1, top, jnp.maximum(low, CHUNK_TILES * n + CHUNK_TILES + 1 - stage))

        return jnp.where(k == 0, low, reach(k - 1)), reach(k)

    @pl.loop(0, chunks)
    def _(k):
        whole(k).wait_recv()

        lo, hi = bounds(k, 0)

        @pl.loop(lo, hi)
        def _(e):
            for p in range(2):
                for j in range(cols):
                    r, c = native(e, j)
                    recip[p, j, at(e), :] = b_ext[p, r, c] * recip[p, j, at(e), :]

        clear_ends(recip, lo, hi)
        first_three(recip, mids, *bounds(k, 1))
        lo, hi = bounds(k, 2)
        fourth(mids, lo, hi, put_u_out)
        clear_ends(vals, lo, hi)
        first_three(vals, mids2, *bounds(k, 3))
        fourth(mids2, *bounds(k, 4), put_v_out)

    @pl.when(has_up)
    def _():
        for c in to_up:
            c.wait_send()

    @pl.when(has_dn)
    def _():
        for c in to_dn:
            c.wait_send()

    for k in range(chunks):
        whole(k).wait_send()


def per_device(snapshots, coefficients):
    tm, space = lax.axis_size("tm"), lax.axis_size("space")
    planes, height, width = coefficients.shape
    cols = width // LANES
    chunks = height // (TILE * CHUNK_TILES)
    wide = (planes, height + 2 * TILE, width)
    field = pltpu.VMEM((planes, cols, height + 4 * TILE, LANES), jnp.float32)
    copies = 6 + chunks

    def kernel(*refs):
        body(tm, space, *refs)

    u, v = pl.pallas_call(
        kernel,
        out_shape=[jax.ShapeDtypeStruct(wide, jnp.float32)] * 2,
        in_specs=[pl.BlockSpec(memory_space=pltpu.HBM)] * 2,
        out_specs=[pl.BlockSpec(memory_space=pltpu.VMEM)] * 2,
        scratch_shapes=[pltpu.VMEM(wide, jnp.float32)] * 3
        + [field] * 6
        + [pltpu.VMEM((cols, height + 4 * TILE, LANES), jnp.float32), field]
        + [pltpu.SemaphoreType.DMA((2,)), pltpu.SemaphoreType.DMA((copies,)), pltpu.SemaphoreType.DMA((copies,))],
        compiler_params=pltpu.CompilerParams(collective_id=0, has_side_effects=True, vmem_limit_bytes=61 * 2**20),
        name="sinkhorn",
    )(snapshots, coefficients)
    inner = slice(TILE, TILE + height)
    return u[None, :, inner], v[None, :, inner]


def solution(mesh):
    placed = (P("tm", None, "space", None), P(None, "space", None))
    return jax.shard_map(
        per_device,
        mesh=mesh,
        in_specs=placed,
        out_specs=(P("tm", None, "space", None), P("tm", None, "space", None)),
        check_vma=False,
    )
```

time: 116 us -> 54.7 us (0.47)
  starting transfers between devices: 69.1 us -> 0 us
  Pallas kernels: 0 us -> 50.8 us
  waiting for transfers between devices: 27.6 us -> 0 us
  other arithmetic: 16.4 us -> 0 us
  local copies, waits for them, and re-layouts: 1.02 us -> 3.11 us
    ppermute x19 -> x0, starting transfers between devices: 69.1 us -> none  [the longest x9 31.5 us: with_halo(): lax.ppermute(head, axis, [((i + 1) % count, i) for i in range(ends)])]
    pallas_call x0 -> x1, Pallas kernels: none -> 50.8 us  [per_device(): pl.pallas_call(kernel, out_shape=[jax.ShapeDtypeStruct(wide, jnp.float32)...]
    ppermute x19 -> x0, waiting for transfers between devices: 27.6 us -> none  [the longest x9 26.2 us: with_halo(): lax.ppermute(tail, axis, [(i, (i + 1) % count) for i in range(ends)])]
    add x11 -> x0, other arithmetic: 9.74 us -> none  [the longest x8 7.7 us: side_sweep(): return values + tau_side * flux_sum]
    broadcast_in_dim x0 -> x1, local copies, waits for them, and re-layouts: none -> 3.11 us  [per_device(): return (u[None, :, inner], v[None, :, inner])]
    another operation x1 -> x0, other arithmetic: 2.67 us -> none  [row_sweep(): return center + tau_rows * flux_sum]
    div x3 -> x0, other arithmetic: 2.26 us -> none  [the longest x2 1.51 us: per_device(): u_part = density / apply_kernel(v_part, coef_wide)]
    broadcast_in_dim x1 -> x0, other arithmetic: 1.72 us -> none  [per_device(): return (u_part[None], v_part[None])]
  transfers between devices with their start and end apart: 19 -> 0, of which waited for: 7 -> 0; matrix products, arithmetic and copies ran while one was open for 2% -> 0% of each run, Pallas kernels for 0% -> 0%
where the time goes in v1:
time: 54.7 us; the launch traced here: 54.5 us
  Pallas kernels  50.8 us (93%)
  local copies, waits for them, and re-layouts  3.11 us (6%)
  between operations  0.64 us (1%)
    pallas_call x1, Pallas kernels, per_device(): pl.pallas_call(kernel, out_shape=[jax.ShapeDtypeStruct(wide, jnp.float32)...  50.8 us
    broadcast_in_dim x1, local copies, waits for them, and re-layouts, per_device(): return (u[None, :, inner], v[None, :, inner])  3.11 us

profile of v1, /device:TPU:8, one launch (start us, length us, event | category | flops | bytes accessed | tf_op | source)
XLA Modules:
  0.0 54.5 jit_solution(7435299544797819481)
XLA Ops:
  0.6 50.8 %sinkhorn.1 = (f32[2,144,1024]{2,1,0:T(8,128)}, f32[2,144,1024]{2,1,0:T(8,128)}) custom-call(f32[1,2,128,1024]{3,2,1,0:T(8,128)} %refs_0_.1, f32[2,128,1024]{2,1,0:T(8,128)} %refs_1_.1), custom_call_target="tpu_custom_call" | custom-call | tf_op jit(solution)/shard_map/sinkhorn/pallas_call | solution.py:305
  51.4 3.1 %slice_bitcast_fusion = (f32[1,2,128,1024]{3,2,1,0:T(8,128)}, f32[1,2,128,1024]{3,2,1,0:T(8,128)}) fusion(f32[2,144,1024]{2,1,0:T(8,128)} %get-tuple-element.5, f32[2,144,1024]{2,1,0:T(8,128)} %get-tuple-element.4), kind=kLoop, calls=%fused_computation | loop fusion | bytes 4194304 | tf_op jit(solution)/shard_map/broadcast_in_dim | solution.py:318

commit v2 on v0

v2 whole, which is shorter than its diff:
```python
import jax
import jax.numpy as jnp
from jax import lax
from jax.experimental import pallas as pl
from jax.experimental.pallas import tpu as pltpu
from jax.sharding import PartitionSpec as P

MESH = pl.DeviceIdType.MESH
TILE = 8
LANES = 128
PAD = 2 * TILE
GROUP = 3
SPAN = GROUP * TILE
TAU_ROWS = 0.25
TAU_SIDE = 0.125


def body(
    tm,
    space,
    snap,
    coef,
    u_out,
    v_out,
    a_ext,
    b_ext,
    c_ext,
    c_str,
    a_str,
    b_str,
    ones,
    first_u,
    first_v,
    second_u,
    second_v,
    mid_a,
    mid_b,
    recip,
    g_row,
    g_right,
    g_left,
    keep,
    g_pl,
    loc_sem,
    snd,
    rcv,
):
    t, s = lax.axis_index("tm"), lax.axis_index("space")
    ahead, behind = lax.rem(t + 1, tm), lax.rem(t + tm - 1, tm)
    has_up, has_dn = s > 0, s < space - 1
    up, dn = jnp.maximum(s - 1, 0), jnp.minimum(s + 1, space - 1)
    height, width = coef.shape[1], coef.shape[2]
    cols = width // LANES
    tiles = height // TILE + 2
    steps = tiles // GROUP
    both = [(p, j) for p in range(2) for j in range(cols)]

    load_c = pltpu.make_async_copy(coef, c_ext.at[:, pl.ds(TILE, height)], loc_sem.at[0])
    load_a = pltpu.make_async_copy(snap.at[0], a_ext.at[:, pl.ds(TILE, height)], loc_sem.at[1])
    load_c.start()
    load_a.start()

    barrier = pltpu.get_barrier_semaphore()

    def greet(dst_t, dst_s):
        pl.semaphore_signal(barrier, inc=1, device_id={"tm": dst_t, "space": dst_s}, device_id_type=MESH)

    greet(ahead, s)

    @pl.when(has_up)
    def _():
        greet(t, up)
        greet(ahead, up)

    @pl.when(has_dn)
    def _():
        greet(t, dn)
        greet(ahead, dn)

    pl.semaphore_wait(barrier, 1 + 2 * has_up.astype(jnp.int32) + 2 * has_dn.astype(jnp.int32))

    def send(i, src, dst, dst_t, dst_s):
        return pltpu.make_async_remote_copy(
            src_ref=src,
            dst_ref=dst,
            send_sem=snd.at[i],
            recv_sem=rcv.at[i],
            device_id={"tm": dst_t, "space": dst_s},
            device_id_type=MESH,
        )

    first, last = pl.ds(0, TILE), pl.ds(height - TILE, TILE)
    head, tail = pl.ds(0, TILE), pl.ds(height + TILE, TILE)
    to_up = [
        send(0, coef.at[:, first], c_ext.at[:, tail], t, up),
        send(1, snap.at[0, :, first], a_ext.at[:, tail], t, up),
        send(2, snap.at[0, :, first], b_ext.at[:, tail], behind, up),
    ]
    to_dn = [
        send(3, coef.at[:, last], c_ext.at[:, head], t, dn),
        send(4, snap.at[0, :, last], a_ext.at[:, head], t, dn),
        send(5, snap.at[0, :, last], b_ext.at[:, head], behind, dn),
    ]

    def part(k, size):
        return send(
            6 + k, snap.at[0, :, pl.ds(k * SPAN, size)], b_ext.at[:, pl.ds(k * SPAN + TILE, size)], behind, s
        )

    parts = [part(k, min(SPAN, height - k * SPAN)) for k in range(steps)]
    for n in range(3):

        @pl.when(has_up)
        def _():
            to_up[n].start()

        @pl.when(has_dn)
        def _():
            to_dn[n].start()

    for copy in parts:
        copy.start()

    def halo_arrived(n):
        @pl.when(has_up)
        def _():
            to_dn[n].wait_recv()

        @pl.when(has_dn)
        def _():
            to_up[n].wait_recv()

    lane = lax.broadcasted_iota(jnp.int32, (TILE, LANES), 1)
    is_first, is_last = lane == 0, lane == LANES - 1
    zeros = jnp.zeros((TILE, LANES), jnp.float32)

    def at(row, shift=0):
        return pl.ds(row + (PAD + shift), TILE)

    def tile(e):
        return pl.ds(pl.multiple_of(TILE * e, TILE), TILE)

    def clear_top(ref):
        @pl.when(jnp.logical_not(has_up))
        def _():
            for p, j in both:
                ref[p, j, at(0), :] = zeros

    def clear_end(ref):
        @pl.when(jnp.logical_not(has_dn))
        def _():
            for p, j in both:
                ref[p, j, at(height + TILE), :] = zeros

    def from_right(x, j):
        return pltpu.roll(jnp.where(is_first, x[(j + 1) % cols], x[j]), LANES - 1, 1)

    def from_left(x, j):
        return pltpu.roll(jnp.where(is_last, x[j - 1], x[j]), 1, 1)

    def row_pass(src, p, j, row):
        mid = src[p, j, at(row), :]
        below = g_row[p, j, at(row), :] * (src[p, j, at(row, 1), :] - mid)
        above = g_row[p, j, at(row, -1), :] * (mid - src[p, j, at(row, -1), :])
        return mid + (below - above)

    def side_pass(x, row):
        out = []
        for p in range(2):
            right = [from_right(x[p], j) for j in range(cols)]
            left = [from_left(x[p], j) for j in range(cols)]
            out.append(
                [
                    (keep[p, j, at(row), :] * x[p][j] + g_pl[j, at(row), :] * x[1 - p][j])
                    + (g_right[p, j, at(row), :] * right[j] + g_left[p, j, at(row), :] * left[j])
                    for j in range(cols)
                ]
            )
        return out

    def first_three(src, dst, row, n=GROUP):
        rows = [row + TILE * i for i in range(n)]
        x = [[[row_pass(src, p, j, r) for j in range(cols)] for p in range(2)] for r in rows]
        x = [side_pass(y, r) for y, r in zip(x, rows)]
        x = [side_pass(y, r) for y, r in zip(x, rows)]
        for y, r in zip(x, rows):
            for p, j in both:
                dst[p, j, at(r), :] = y[p][j]

    def fourth(src, num, dst, row, n=GROUP):
        for i in range(n):
            r = row + TILE * i
            for p, j in both:
                den = row_pass(src, p, j, r)
                dst[p, j, at(r), :] = (1.0 if num is None else num[p, j, at(r), :]) / den

    def strip(src, dst, e):
        for p, j in both:
            dst[p, j, at(TILE * e), :] = src[p, tile(e), pl.ds(LANES * j, LANES)]

    def weigh(e):
        row = TILE * e
        c = [[c_str[p, j, at(row), :] for j in range(cols)] for p in range(2)]
        for j in range(cols):
            g_pl[j, at(row), :] = (0.5 * TAU_SIDE) * (c[0][j] + c[1][j])
        for p in range(2):
            walls = [(0.5 * TAU_SIDE) * c[p][j] for j in range(cols)]
            right = [walls[j] + from_right(walls, j) for j in range(cols)]
            right[-1] = jnp.where(is_last, 0.0, right[-1])
            for j in range(cols):
                left = from_left(right, j)
                kept = 1.0 - walls[j] - (0.5 * TAU_SIDE) * (c[0][j] + c[1][j]) - right[j] - left
                if j == 0:
                    kept = jnp.where(is_first, kept - walls[j], kept)
                if j == cols - 1:
                    kept = jnp.where(is_last, kept - walls[j], kept)
                g_right[p, j, at(row), :] = right[j]
                g_left[p, j, at(row), :] = left
                keep[p, j, at(row), :] = kept
                g_row[p, j, at(row), :] = (0.5 * TAU_ROWS) * (c[p][j] + c_str[p, j, at(row, 1), :])

    @pl.loop(0, tiles)
    def _(e):
        for p, j in both:
            ones[p, j, at(TILE * e), :] = zeros + 1.0

    clear_top(ones)
    clear_end(ones)
    load_c.wait()

    @pl.loop(1, tiles - 1)
    def _(e):
        strip(c_ext, c_str, e)

    @pl.loop(1, tiles - 1, unroll=2)
    def _(e):
        weigh(e)

    inner = steps - 1
    gap = (tiles * TILE - inner * SPAN) // 2

    @pl.loop(0, inner)
    def _(g):
        first_three(ones, mid_a, gap + SPAN * g)

    load_a.wait()

    @pl.loop(1, tiles - 1)
    def _(e):
        strip(a_ext, a_str, e)

    halo_arrived(0)

    @pl.when(jnp.logical_not(has_up))
    def _():
        c_ext[:, head, :] = jnp.zeros((2, TILE, width), jnp.float32)

    @pl.when(jnp.logical_not(has_dn))
    def _():
        c_ext[:, tail, :] = jnp.zeros((2, TILE, width), jnp.float32)

    for e in (0, tiles - 1):
        strip(c_ext, c_str, e)
    for e in (0, tiles - 2, tiles - 1):
        weigh(e)
    first_three(ones, mid_a, gap - SPAN)
    first_three(ones, mid_a, tiles * TILE - gap)
    clear_top(mid_a)
    clear_end(mid_a)
    halo_arrived(1)
    for e in (0, tiles - 1):
        strip(a_ext, a_str, e)

    @pl.loop(0, steps)
    def _(g):
        fourth(mid_a, a_str, first_u, SPAN * g)

    clear_top(first_u)
    clear_end(first_u)

    @pl.loop(0, steps)
    def _(g):
        first_three(first_u, mid_b, SPAN * g)

    clear_top(mid_b)
    clear_end(mid_b)

    @pl.loop(0, steps)
    def _(g):
        fourth(mid_b, None, recip, SPAN * g)

    def scale(e, n):
        for i in range(n):
            for p, j in both:
                b = b_ext[p, tile(e + i), pl.ds(LANES * j, LANES)]
                b_str[p, j, at(TILE * (e + i)), :] = b
                first_v[p, j, at(TILE * (e + i)), :] = b * recip[p, j, at(TILE * (e + i)), :]

    def give(e, n):
        for i in range(n):
            for p, j in both:
                where = pl.ds(pl.multiple_of(TILE * (e + i - 1), TILE), TILE), pl.ds(LANES * j, LANES)
                u_out[0, p, where[0], where[1]] = second_u[p, j, at(TILE * (e + i)), :]
                v_out[0, p, where[0], where[1]] = second_v[p, j, at(TILE * (e + i)), :]

    def trail(end, n, clear):
        first_three(first_v, mid_a, end + 3 - TILE * n, n)
        clear(mid_a)
        fourth(mid_a, a_str, second_u, end + 2 - SPAN)
        clear(second_u)
        first_three(second_u, mid_b, end + 1 - SPAN)
        clear(mid_b)
        fourth(mid_b, b_str, second_v, end - SPAN)

    def step(e, n, end, out, n_out, clear):
        scale(e, n)
        clear(first_v)
        trail(end, n, clear)
        give(out, n_out)

    halo_arrived(2)
    parts[0].wait_recv()
    step(0, GROUP + 1, SPAN + 4, 1, GROUP - 1, clear_top)

    @pl.loop(1, steps - 1)
    def _(k):
        part(k, SPAN).wait_recv()
        step(GROUP * k + 1, GROUP, SPAN * k + (SPAN + 4), GROUP * k, GROUP, lambda ref: None)

    parts[-1].wait_recv()
    step(tiles - GROUP, GROUP, height + TILE, tiles - GROUP - 1, GROUP, clear_end)

    @pl.when(has_up)
    def _():
        for copy in to_up:
            copy.wait_send()

    @pl.when(has_dn)
    def _():
        for copy in to_dn:
            copy.wait_send()

    for copy in parts:
        copy.wait_send()


def per_device(snapshots, coefficients):
    tm, space = lax.axis_size("tm"), lax.axis_size("space")
    planes, height, width = coefficients.shape
    cols = width // LANES
    rows = height + 2 * TILE
    wide = (planes, rows, width)
    field = pltpu.VMEM((planes, cols, rows + 2 * PAD, LANES), jnp.float32)
    copies = 6 + rows // SPAN

    def kernel(*refs):
        body(tm, space, *refs)

    return pl.pallas_call(
        kernel,
        out_shape=[jax.ShapeDtypeStruct(snapshots.shape, jnp.float32)] * 2,
        in_specs=[pl.BlockSpec(memory_space=pltpu.HBM)] * 2,
        out_specs=[pl.BlockSpec(memory_space=pltpu.VMEM)] * 2,
        scratch_shapes=[pltpu.VMEM(wide, jnp.float32)] * 3
        + [field] * 15
        + [pltpu.VMEM((cols, rows + 2 * PAD, LANES), jnp.float32)]
        + [pltpu.SemaphoreType.DMA((2,)), pltpu.SemaphoreType.DMA((copies,)), pltpu.SemaphoreType.DMA((copies,))],
        compiler_params=pltpu.CompilerParams(collective_id=0, has_side_effects=True, vmem_limit_bytes=60 * 2**20),
        name="sinkhorn",
    )(snapshots, coefficients)


def solution(mesh):
    placed = (P("tm", None, "space", None), P(None, "space", None))
    return jax.shard_map(
        per_device,
        mesh=mesh,
        in_specs=placed,
        out_specs=(P("tm", None, "space", None), P("tm", None, "space", None)),
        check_vma=False,
    )
```

time: 116 us -> 33.3 us (0.29)
  starting transfers between devices: 69.1 us -> 0 us
  Pallas kernels: 0 us -> 29.1 us
  waiting for transfers between devices: 27.6 us -> 0 us
  other arithmetic: 16.4 us -> 0 us
  local copies, waits for them, and re-layouts: 1.02 us -> 3.37 us
    ppermute x19 -> x0, starting transfers between devices: 69.1 us -> none  [the longest x9 31.5 us: with_halo(): lax.ppermute(head, axis, [((i + 1) % count, i) for i in range(ends)])]
    pallas_call x0 -> x1, Pallas kernels: none -> 29.1 us  [per_device(): pl.pallas_call(kernel, out_shape=[jax.ShapeDtypeStruct(snapshots.shape, j...]
    ppermute x19 -> x0, waiting for transfers between devices: 27.6 us -> none  [the longest x9 26.2 us: with_halo(): lax.ppermute(tail, axis, [(i, (i + 1) % count) for i in range(ends)])]
    add x11 -> x0, other arithmetic: 9.74 us -> none  [the longest x8 7.7 us: side_sweep(): return values + tau_side * flux_sum]
    unnamed x6 -> x4, local copies, waits for them, and re-layouts: 0.02 us -> 3.37 us
    another operation x1 -> x0, other arithmetic: 2.67 us -> none  [row_sweep(): return center + tau_rows * flux_sum]
    div x3 -> x0, other arithmetic: 2.26 us -> none  [the longest x2 1.51 us: per_device(): u_part = density / apply_kernel(v_part, coef_wide)]
    broadcast_in_dim x1 -> x0, other arithmetic: 1.72 us -> none  [per_device(): return (u_part[None], v_part[None])]
  transfers between devices with their start and end apart: 19 -> 0, of which waited for: 7 -> 0; matrix products, arithmetic and copies ran while one was open for 2% -> 0% of each run, Pallas kernels for 0% -> 0%
where the time goes in v2:
time: 33.3 us; the launch traced here: 33.1 us
  Pallas kernels  29.1 us (87%)
  local copies, waits for them, and re-layouts  3.37 us (10%)
  between operations  0.65 us (2%)
    pallas_call x1, Pallas kernels, per_device(): pl.pallas_call(kernel, out_shape=[jax.ShapeDtypeStruct(snapshots.shape, j...  29.1 us
    unnamed x4, local copies, waits for them, and re-layouts  3.37 us

profile of v2, /device:TPU:8, one launch (start us, length us, event | category | flops | bytes accessed | tf_op | source)
XLA Modules:
  0.0 33.1 jit_solution(14714430711515606983)
XLA Ops:
  0.6 29.1 %sinkhorn.1 = (f32[1,2,128,1024]{3,2,1,0:T(8,128)}, f32[1,2,128,1024]{3,2,1,0:T(8,128)}) custom-call(f32[1,2,128,1024]{3,2,1,0:T(8,128)} %refs_0_.1, f32[2,128,1024]{2,1,0:T(8,128)} %refs_1_.1), custom_call_target="tpu_custom_call" | custom-call | tf_op jit(solution)/shard_map/sinkhorn/pallas_call | solution.py:359
  29.8 0.0 copy-start
  29.8 2.4 %copy.6 = f32[1,2,128,1024]{3,2,1,0:T(8,128)} copy(f32[1,2,128,1024]{3,2,1,0:T(8,128)} %get-tuple-element.4) | data formatting | bytes 2097152
  32.2 0.0 copy-done
  32.2 1.0 %copy.7 = f32[1,2,128,1024]{3,2,1,0:T(8,128)} copy(f32[1,2,128,1024]{3,2,1,0:T(8,128)S(1)} %copy-done) | data formatting | bytes 2097152
Async XLA Ops:
  29.8 2.4 %copy-start = (f32[1,2,128,1024]{3,2,1,0:T(8,128)S(1)}, f32[1,2,128,1024]{3,2,1,0:T(8,128)}, u32[]{:S(2)}) copy-start(f32[1,2,128,1024]{3,2,1,0:T(8,128)} %get-tuple-element.5) | copy-start | bytes 3145732

commit v3 on v2

v3 whole, which is shorter than its diff:
```python
import jax
import jax.numpy as jnp
from jax import lax
from jax.experimental import pallas as pl
from jax.experimental.pallas import tpu as pltpu
from jax.sharding import PartitionSpec as P

MESH = pl.DeviceIdType.MESH
TILE = 8
LANES = 128
PAD = 2 * TILE
GROUP = 3
SPAN = GROUP * TILE
STOP = 3
OWN = 3
GO = 1
GO_STEP = 3
TAU_ROWS = 0.25
TAU_SIDE = 0.125


def body(
    tm,
    space,
    snap,
    coef,
    u_out,
    v_out,
    a_ext,
    b_ext,
    c_ext,
    c_str,
    a_str,
    b_str,
    ones,
    first_u,
    first_v,
    second_u,
    second_v,
    mid_a,
    mid_b,
    recip,
    row_b,
    side_b,
    row_d,
    side_d,
    g_row,
    g_right,
    g_left,
    keep,
    g_pl,
    hop,
    loc_sem,
    snd,
    rcv,
    hop_snd,
    hop_rcv,
    on_snd,
    ready,
    ready_via,
    ready_go,
    go,
):
    t, s = lax.axis_index("tm"), lax.axis_index("space")
    ahead, behind = lax.rem(t + 1, tm), lax.rem(t + tm - 1, tm)
    has_up, has_dn = s > 0, s < space - 1
    up, dn = jnp.maximum(s - 1, 0), jnp.minimum(s + 1, space - 1)
    height, width = coef.shape[1], coef.shape[2]
    cols = width // LANES
    tiles = height // TILE + 2
    sweep = tiles // GROUP
    steps = height // SPAN
    both = [(p, j) for p in range(2) for j in range(cols)]

    load_c = pltpu.make_async_copy(coef, c_ext.at[:, pl.ds(TILE, height)], loc_sem.at[0])
    load_a = pltpu.make_async_copy(snap.at[0], a_ext.at[:, pl.ds(TILE, height)], loc_sem.at[1])

    half = tm // 2
    stop = 2 * max(1, half // 2 * STOP // 16)
    place = lax.rem(t, half)
    is_src, is_via, is_dst = place == 0, place == stop, place == half - 1

    def ahead_by(n):
        return lax.rem(t + (n + tm) % tm, tm)

    t_partner, t_via, t_far_via = ahead_by(half), ahead_by(stop), ahead_by(half + stop)

    barrier = pltpu.get_barrier_semaphore()

    def tell(sem, dst_t, dst_s):
        pl.semaphore_signal(sem, inc=1, device_id={"tm": dst_t, "space": dst_s}, device_id_type=MESH)

    @pl.when(has_up)
    def _():
        tell(barrier, t, up)

    @pl.when(has_dn)
    def _():
        tell(barrier, t, dn)

    @pl.when(jnp.logical_not(is_dst))
    def _():
        tell(barrier, ahead, s)

        @pl.when(has_up)
        def _():
            tell(barrier, ahead, up)

        @pl.when(has_dn)
        def _():
            tell(barrier, ahead, dn)

    @pl.when(is_src)
    def _():
        tell(barrier, t_partner, s)
        tell(barrier, t_via, s)
        tell(barrier, t_far_via, s)
        tell(barrier, ahead_by(half - 1), s)

    @pl.when(is_via)
    def _():
        tell(barrier, ahead_by(half - 1 - stop), s)

    load_c.start()
    load_a.start()
    beside = has_up.astype(jnp.int32) + has_dn.astype(jnp.int32)
    before = jnp.where(is_src, 1, 1 + beside)
    on_way = jnp.where(jnp.logical_or(is_dst, is_via), 2, 0)
    pl.semaphore_wait(barrier, beside + before + on_way)

    @pl.when(is_via)
    def _():
        tell(ready_via, ahead_by(half - stop), s)
        tell(ready_go, ahead_by(-stop), s)

    @pl.when(is_dst)
    def _():
        tell(ready, ahead_by(1 - half), s)
        tell(ready, ahead_by(1 - half + stop), s)

    def send(i, src, dst, dst_t, dst_s, sent=None):
        return pltpu.make_async_remote_copy(
            src_ref=src,
            dst_ref=dst,
            send_sem=snd.at[i if sent is None else sent],
            recv_sem=rcv.at[i],
            device_id={"tm": dst_t, "space": dst_s},
            device_id_type=MESH,
        )

    first, last = pl.ds(TILE, TILE), pl.ds(height, TILE)
    head, tail = pl.ds(0, TILE), pl.ds(height + TILE, TILE)
    to_up = [
        send(0, c_ext.at[:, first], c_ext.at[:, tail], t, up),
        send(1, a_ext.at[:, first], a_ext.at[:, tail], t, up),
        send(2, a_ext.at[:, first], b_ext.at[:, tail], behind, up),
    ]
    to_dn = [
        send(3, c_ext.at[:, last], c_ext.at[:, head], t, dn),
        send(4, a_ext.at[:, last], a_ext.at[:, head], t, dn),
        send(5, a_ext.at[:, last], b_ext.at[:, head], behind, dn),
    ]

    b_beside = [
        send(2, b_ext.at[:, first], b_ext.at[:, tail], t, up, 6 + steps),
        send(5, b_ext.at[:, last], b_ext.at[:, head], t, dn, 7 + steps),
    ]

    def part(k, size):
        rows = pl.ds(k * SPAN + TILE, size)
        return send(6 + k, a_ext.at[:, rows], b_ext.at[:, rows], behind, s)

    parts = [part(k, SPAN if k < steps - 1 else height - k * SPAN) for k in range(steps)]

    def start_beside(n):
        @pl.when(has_up)
        def _():
            to_up[n].start()

        @pl.when(has_dn)
        def _():
            to_dn[n].start()

    load_c.wait()
    start_beside(0)
    load_a.wait()
    start_beside(1)

    @pl.when(jnp.logical_not(is_src))
    def _():
        start_beside(2)
        for copy in parts:
            copy.start()

    def legs(k, n):
        lo, size = k * SPAN + TILE, SPAN
        if k == steps:
            lo, size = height, TILE
        src, dst, dst_t, sent = (
            (a_ext, hop, t_partner, hop_snd),
            (a_ext, hop, t_far_via, hop_snd),
            (hop, b_ext, ahead_by(half - 1), on_snd),
            (hop, b_ext, ahead_by(half - 1 - stop), on_snd),
        )[n]
        rows = pl.ds(lo, size)
        return pltpu.make_async_remote_copy(
            src_ref=src.at[:, rows],
            dst_ref=dst.at[:, rows],
            send_sem=sent.at[k],
            recv_sem=hop_rcv.at[k],
            device_id={"tm": dst_t, "space": s},
            device_id_type=MESH,
        )

    own, by_via = (steps, *range(OWN)), range(OWN, steps)

    @pl.when(is_src)
    def _():
        for k in own:
            legs(k, 0).start()

    def pass_on(here, chunks, n):
        @pl.when(here)
        def _():
            pl.semaphore_wait(ready, 1)
            for k in chunks:
                legs(k, n).wait_recv()
                legs(k, n).start()

    def arrived(k):
        @pl.when(is_dst)
        def _():
            if k:
                legs(k, 2).wait_recv()

        @pl.when(jnp.logical_not(is_dst))
        def _():
            parts[k].wait_recv()

    def halo_arrived(n):
        @pl.when(has_up)
        def _():
            to_dn[n].wait_recv()

        @pl.when(has_dn)
        def _():
            to_up[n].wait_recv()

    lane = lax.broadcasted_iota(jnp.int32, (TILE, LANES), 1)
    is_first, is_last = lane == 0, lane == LANES - 1
    zeros = jnp.zeros((TILE, LANES), jnp.float32)

    def at(row, shift=0):
        return pl.ds(row + (PAD + shift), TILE)

    def tile(e):
        return pl.ds(pl.multiple_of(TILE * e, TILE), TILE)

    def clear_top(ref):
        @pl.when(jnp.logical_not(has_up))
        def _():
            for p, j in both:
                ref[p, j, at(0), :] = zeros

    def clear_end(ref):
        @pl.when(jnp.logical_not(has_dn))
        def _():
            for p, j in both:
                ref[p, j, at(height + TILE), :] = zeros

    def from_right(x, j):
        return pltpu.roll(jnp.where(is_first, x[(j + 1) % cols], x[j]), LANES - 1, 1)

    def from_left(x, j):
        return pltpu.roll(jnp.where(is_last, x[j - 1], x[j]), 1, 1)

    def row_pass(src, p, j, row):
        mid = src[p, j, at(row), :]
        below = g_row[p, j, at(row), :] * (src[p, j, at(row, 1), :] - mid)
        above = g_row[p, j, at(row, -1), :] * (mid - src[p, j, at(row, -1), :])
        return mid + (below - above)

    def side_pass(src, dst, row):
        for p in range(2):
            for j in range(cols):
                mid = src[p, j, at(row), :]
                right = jnp.where(is_first, src[p, (j + 1) % cols, at(row), :], mid)
                left = jnp.where(is_last, src[p, (j - 1) % cols, at(row), :], mid)
                dst[p, j, at(row), :] = (
                    keep[p, j, at(row), :] * mid + g_pl[j, at(row), :] * src[1 - p, j, at(row), :]
                ) + (
                    g_right[p, j, at(row), :] * pltpu.roll(right, LANES - 1, 1)
                    + g_left[p, j, at(row), :] * pltpu.roll(left, 1, 1)
                )

    def first_three(*runs):
        for src, row_tmp, _, _, rows in runs:
            for r in rows:
                for p, j in both:
                    row_tmp[p, j, at(r), :] = row_pass(src, p, j, r)
        for _, row_tmp, side_tmp, _, rows in runs:
            for r in rows:
                side_pass(row_tmp, side_tmp, r)
        for _, _, side_tmp, dst, rows in runs:
            for r in rows:
                side_pass(side_tmp, dst, r)

    def run(row, n):
        return [row + TILE * i for i in range(n)]

    def fourth(src, num, dst, row, n=GROUP):
        for i in range(n):
            r = row + TILE * i
            for p, j in both:
                den = row_pass(src, p, j, r)
                dst[p, j, at(r), :] = (1.0 if num is None else num[p, j, at(r), :]) / den

    def strip(src, dst, e):
        for p, j in both:
            dst[p, j, at(TILE * e), :] = src[p, tile(e), pl.ds(LANES * j, LANES)]

    def weigh(e):
        row = TILE * e
        c = [[c_str[p, j, at(row), :] for j in range(cols)] for p in range(2)]
        for j in range(cols):
            g_pl[j, at(row), :] = (0.5 * TAU_SIDE) * (c[0][j] + c[1][j])
        for p in range(2):
            walls = [(0.5 * TAU_SIDE) * c[p][j] for j in range(cols)]
            right = [walls[j] + from_right(walls, j) for j in range(cols)]
            right[-1] = jnp.where(is_last, 0.0, right[-1])
            for j in range(cols):
                left = from_left(right, j)
                kept = 1.0 - walls[j] - (0.5 * TAU_SIDE) * (c[0][j] + c[1][j]) - right[j] - left
                if j == 0:
                    kept = jnp.where(is_first, kept - walls[j], kept)
                if j == cols - 1:
                    kept = jnp.where(is_last, kept - walls[j], kept)
                g_right[p, j, at(row), :] = right[j]
                g_left[p, j, at(row), :] = left
                keep[p, j, at(row), :] = kept
                g_row[p, j, at(row), :] = (0.5 * TAU_ROWS) * (c[p][j] + c_str[p, j, at(row, 1), :])

    @pl.loop(0, tiles)
    def _(e):
        for p, j in both:
            ones[p, j, at(TILE * e), :] = zeros + 1.0

    clear_top(ones)
    clear_end(ones)
    @pl.loop(1, tiles - 1)
    def _(e):
        strip(c_ext, c_str, e)

    @pl.loop(1, tiles - 1, unroll=2)
    def _(e):
        weigh(e)

    inner = sweep - 1
    gap = (tiles * TILE - inner * SPAN) // 2

    @pl.loop(0, GROUP)
    def _(g):
        first_three((ones, row_b, side_b, mid_a, run(gap + TILE * inner * g, inner)))

    @pl.loop(1, tiles - 1)
    def _(e):
        strip(a_ext, a_str, e)

    halo_arrived(0)

    @pl.when(jnp.logical_not(has_up))
    def _():
        c_ext[:, head, :] = jnp.zeros((2, TILE, width), jnp.float32)

    @pl.when(jnp.logical_not(has_dn))
    def _():
        c_ext[:, tail, :] = jnp.zeros((2, TILE, width), jnp.float32)

    for e in (0, tiles - 1):
        strip(c_ext, c_str, e)
    for e in (0, tiles - 2, tiles - 1):
        weigh(e)
    first_three((ones, row_b, side_b, mid_a, run(gap - SPAN, GROUP) + run(tiles * TILE - gap, GROUP)))
    clear_top(mid_a)
    clear_end(mid_a)
    halo_arrived(1)

    for e in (0, tiles - 1):
        strip(a_ext, a_str, e)

    @pl.loop(0, sweep)
    def _(g):
        fourth(mid_a, a_str, first_u, SPAN * g)

    clear_top(first_u)
    clear_end(first_u)

    @pl.when(is_src)
    def _():
        pl.semaphore_wait(ready_via, 1)
        for k in by_via:
            legs(k, 1).start()

    @pl.loop(0, GROUP)
    def _(g):
        first_three((first_u, row_b, side_b, mid_b, run(TILE * sweep * g, sweep)))

    clear_top(mid_b)
    clear_end(mid_b)
    pass_on(is_src, own, 2)

    @pl.loop(0, sweep)
    def _(g):
        fourth(mid_b, None, recip, SPAN * g)

    def scale(e, n):
        for i in range(n):
            for p, j in both:
                b = b_ext[p, tile(e + i), pl.ds(LANES * j, LANES)]
                b_str[p, j, at(TILE * (e + i)), :] = b
                first_v[p, j, at(TILE * (e + i)), :] = b * recip[p, j, at(TILE * (e + i)), :]

    ends = [SPAN * k + (SPAN + 4) for k in range(steps - 1)] + [height + TILE]
    sizes = [GROUP] * (steps - 1) + [tiles - 1 - GROUP * (steps - 1)]

    def run_b(k):
        n = sizes[k] + (k == 0)
        return first_v, row_b, side_b, mid_a, run(ends[k] + 3 - TILE * n, n)

    def run_d(k):
        return second_u, row_d, side_d, mid_b, run(ends[k] + 1 - TILE * sizes[k], sizes[k])

    def clear(k, ref):
        if k == 0:
            clear_top(ref)
        if k == steps - 1:
            clear_end(ref)

    def give(src, out, lo, hi):
        for e in range(lo, hi):
            for p, j in both:
                out[0, p, pl.ds(TILE * (e - 1), TILE), pl.ds(LANES * j, LANES)] = src[p, j, at(TILE * e), :]

    def done(k):
        return tiles - 1 if k == steps - 1 else GROUP * (k + 1)

    def finish(k):
        clear(k, mid_b)
        fourth(mid_b, b_str, second_v, ends[k] - TILE * sizes[k], sizes[k])
        give(second_v, v_out, done(k - 1) if k else 1, done(k))

    def step(k):
        scale(0 if k == 0 else GROUP * k + 1, sizes[k] + (k == 0))
        clear(k, first_v)
        if k == 0:
            first_three(run_b(k))
        else:
            first_three(run_b(k), run_d(k - 1))
        clear(k, mid_a)
        fourth(mid_a, a_str, second_u, ends[k] + 2 - TILE * sizes[k], sizes[k])
        clear(k, second_u)
        give(second_u, u_out, done(k - 1) if k else 1, done(k))
        if k:
            finish(k - 1)

    @pl.when(is_dst)
    def _():
        legs(steps, 2).wait_recv()

        @pl.when(has_dn)
        def _():
            b_beside[1].start()

        legs(0, 2).wait_recv()

        @pl.when(has_up)
        def _():
            b_beside[0].start()

    halo_arrived(2)

    for k in range(steps):
        arrived(k)
        if k == GO_STEP:

            @pl.when(is_src)
            def _():
                for n in own[: GO + 1]:
                    legs(n, 2).wait_send()
                pl.semaphore_wait(ready_go, 1)
                tell(go, t_via, s)

        step(k)

    first_three(run_d(steps - 1))
    finish(steps - 1)

    @pl.when(is_via)
    def _():
        pl.semaphore_wait(go, 1)

    pass_on(is_via, by_via, 3)

    for n in range(3):

        @pl.when(has_up if n < 2 else jnp.logical_and(has_up, jnp.logical_not(is_src)))
        def _():
            to_up[n].wait_send()

        @pl.when(has_dn if n < 2 else jnp.logical_and(has_dn, jnp.logical_not(is_src)))
        def _():
            to_dn[n].wait_send()

    @pl.when(jnp.logical_not(is_src))
    def _():
        for copy in parts:
            copy.wait_send()

    @pl.when(jnp.logical_and(is_dst, has_up))
    def _():
        b_beside[0].wait_send()

    @pl.when(jnp.logical_and(is_dst, has_dn))
    def _():
        b_beside[1].wait_send()

    for here, chunks, n in (
        (is_src, own, 0),
        (is_src, by_via, 1),
        (is_src, own[GO + 1 :], 2),
        (is_via, by_via, 3),
    ):

        @pl.when(here)
        def _():
            for k in chunks:
                legs(k, n).wait_send()


def per_device(snapshots, coefficients):
    tm, space = lax.axis_size("tm"), lax.axis_size("space")
    planes, height, width = coefficients.shape
    cols = width // LANES
    rows = height + 2 * TILE
    wide = (planes, rows, width)
    field = pltpu.VMEM((planes, cols, rows + 2 * PAD, LANES), jnp.float32)
    copies = 8 + rows // SPAN

    def kernel(*refs):
        body(tm, space, *refs)

    return pl.pallas_call(
        kernel,
        out_shape=[jax.ShapeDtypeStruct(snapshots.shape, jnp.float32)] * 2,
        in_specs=[pl.BlockSpec(memory_space=pltpu.HBM)] * 2,
        out_specs=[pl.BlockSpec(memory_space=pltpu.VMEM)] * 2,
        scratch_shapes=[pltpu.VMEM(wide, jnp.float32)] * 3
        + [field] * 19
        + [pltpu.VMEM((cols, rows + 2 * PAD, LANES), jnp.float32)]
        + [pltpu.VMEM(wide, jnp.float32)]
        + [pltpu.SemaphoreType.DMA((2,)), pltpu.SemaphoreType.DMA((copies,)), pltpu.SemaphoreType.DMA((copies,))]
        + [pltpu.SemaphoreType.DMA((rows // SPAN + 1,))] * 3
        + [pltpu.SemaphoreType.REGULAR] * 4,
        compiler_params=pltpu.CompilerParams(collective_id=0, has_side_effects=True, vmem_limit_bytes=51 * 2**20),
        name="sinkhorn",
    )(snapshots, coefficients)


def solution(mesh):
    placed = (P("tm", None, "space", None), P(None, "space", None))
    return jax.shard_map(
        per_device,
        mesh=mesh,
        in_specs=placed,
        out_specs=(P("tm", None, "space", None), P("tm", None, "space", None)),
        check_vma=False,
    )
```

time: 33.3 us -> 29.5 us (0.89)
  the two profiles are of different devices: /device:TPU:8 before, /device:TPU:96 now
where the time goes in v3:
time: 29.5 us; the launch traced here: 29.4 us
  Pallas kernels  26.8 us (91%)
  local copies, waits for them, and re-layouts  1.94 us (7%)
  between operations  0.64 us (2%)
    pallas_call x1, Pallas kernels, per_device(): pl.pallas_call(kernel, out_shape=[jax.ShapeDtypeStruct(snapshots.shape, j...  26.8 us
    unnamed x2, local copies, waits for them, and re-layouts  1.94 us

profile of v3, /device:TPU:96, one launch (start us, length us, event | category | flops | bytes accessed | tf_op | source)
XLA Modules:
  0.0 29.4 jit_solution(12502879980270996418)
XLA Ops:
  0.6 26.8 %sinkhorn.1 = (f32[1,2,128,1024]{3,2,1,0:T(8,128)S(1)}, f32[1,2,128,1024]{3,2,1,0:T(8,128)S(1)}) custom-call(f32[1,2,128,1024]{3,2,1,0:T(8,128)} %refs_0_.1, f32[2,128,1024]{2,1,0:T(8,128)} %refs_1_.1), custom_call_target="tpu_custom_call" | custom-call | tf_op jit(solution)/shard_map/sinkhorn/pallas_call | solution.py:552
  27.4 1.0 %copy.6 = f32[1,2,128,1024]{3,2,1,0:T(8,128)} copy(f32[1,2,128,1024]{3,2,1,0:T(8,128)S(1)} %get-tuple-element.4) | data formatting | bytes 2097152
  28.4 1.0 %copy.7 = f32[1,2,128,1024]{3,2,1,0:T(8,128)} copy(f32[1,2,128,1024]{3,2,1,0:T(8,128)S(1)} %get-tuple-element.5) | data formatting | bytes 2097152
